TPU v7x, 512 devices: a whole 4x8x8 slice. The times are simulated.
512 devices in a mesh: wide: 64 (over y, x, core), narrow: 8 (over z).
Axes of the slice: x: 4, y: 8, z: 8, core: 2. Of those that a mesh axis runs over, the one named last changes fastest.
Arguments:
- queries: bfloat16 [65536, 2048], P(('wide', 'narrow')), may hold values from -6 to 6
- keys: bfloat16 [65536, 2048], P(('wide', 'narrow')), may hold values from -6 to 6
- values: bfloat16 [65536, 2048], P(('wide', 'narrow')), may hold values from -6 to 6
- norm_gain: float32 [2048], replicated, may hold values from 0.1 to 1.9
Outputs:
- attended: bfloat16 [65536, 2048], P(('wide', 'narrow'))
All inputs are finite; a program needn't handle non-finite values.
Results may differ from a plain program's by a relative error of at most 0.0032.
Values sent between devices are 32-bit elements; how exact they have to be, the bound alone decides.
No kernel may reach another device: no remote copies, remote signals or barrier semaphores. Data moves between devices by JAX's collectives and lax.ppermute only.
A program may use at most 192 MiB of HBM per device.

v0:
```python
import jax
import jax.numpy as jnp
from jax import lax
from jax.sharding import PartitionSpec as P

H = 16
DK = 128


def carried_in(part, axis, combine, identity):
    place = lax.axis_index(axis)
    gathered = lax.all_gather(part, axis)
    state = jnp.zeros_like(part) + jnp.asarray(identity, part.dtype)

    def one(hop, state):
        return combine(state, lax.dynamic_index_in_dim(gathered, hop, 0, False))

    return lax.fori_loop(0, place, one, state)


def add_states(earlier, later):
    return earlier + later


def local(queries, keys, values, norm_gain):
    tok_rows = queries.shape[0]
    heads = H
    width = DK
    feature_queries = (
        (jax.nn.elu(queries.astype(jnp.float32)) + 1.0)
        .astype(jnp.bfloat16)
        .reshape(tok_rows, heads, width)
    )
    feature_keys = (
        (jax.nn.elu(keys.astype(jnp.float32)) + 1.0)
        .astype(jnp.bfloat16)
        .reshape(tok_rows, heads, width)
    )
    value_rows = values.reshape(tok_rows, heads, width)
    local_state = jnp.einsum(
        "may,mai->ayi", feature_keys, value_rows, preferred_element_type=jnp.float32
    )
    by_block = lax.all_to_all(local_state[None], "narrow", split_axis=1, concat_axis=0, tiled=True)
    running = jnp.cumsum(by_block, axis=0)
    group_sum = running[-1]
    inside = running - by_block
    head_empty = jnp.zeros(group_sum.shape, jnp.float32)
    outside = carried_in(group_sum, "wide", add_states, head_empty)
    block_prefix = inside + outside[None]
    prefix_state = lax.all_to_all(block_prefix, "narrow", split_axis=0, concat_axis=1, tiled=True)[
        0
    ]
    causal = jnp.tril(jnp.ones((tok_rows, tok_rows), jnp.float32))
    scores = jnp.einsum(
        "qhk,shk->hqs", feature_queries, feature_keys, preferred_element_type=jnp.float32
    )
    weights = (scores * causal[None]).astype(jnp.bfloat16)
    inner = jnp.einsum("hqs,shv->qhv", weights, value_rows, preferred_element_type=jnp.float32)
    outer_product = jnp.einsum(
        "dtu,tuj->dtj",
        feature_queries.astype(jnp.float32),
        prefix_state,
        precision=lax.Precision.HIGHEST,
    )
    mixed = inner + outer_product
    meansq = jnp.mean(mixed * mixed, axis=-1, keepdims=True)
    gain = norm_gain.reshape(heads, width)
    result = (gain[None] * mixed * lax.rsqrt(meansq + 1e-05)).astype(jnp.bfloat16)
    return result.reshape(tok_rows, heads * width)


def solution(mesh):
    placed = (
        P(("wide", "narrow"), None),
        P(("wide", "narrow"), None),
        P(("wide", "narrow"), None),
        P(),
    )
    return jax.shard_map(
        local, mesh=mesh, in_specs=placed, out_specs=P(("wide", "narrow"), None), check_vma=False
    )
```

profile of v0, /device:TPU:63, one launch (start us, length us, event | category | flops | bytes accessed | tf_op | source)
XLA Modules:
  0.0 242.6 jit_solution(12066782442210563976)
XLA Ops:
  6.5 1.6 fusion.7
  8.7 37.1 %all_to_all.21 = f32[1,16,128,128]{3,2,0,1:T(8,128)S(1)} all-to-all(f32[1,16,128,128]{3,2,0,1:T(8,128)S(1)} %convolution_bitcast_fusion), channel_id=1, replica_groups=mesh['wide'=64,'narrow'=8] {'narrow'}, dimensions={1} | all-to-all | bytes 2097152 | tf_op jit(solution)/shard_map/all_to_all | solution.py:43
  45.8 1.0 fusion.23
  47.5 84.0 %all-gather.2.cloned.1.call-done = f32[64,2,128,128]{3,2,1,0:T(8,128)} async-done(((f32[1,2,128,128]{3,2,1,0:T(8,128)}), f32[64,2,128,128]{3,2,1,0:T(8,128)}) %all-gather.2.cloned.1.call-update) | async-done | bytes 8388624 | tf_op jit(solution)/shard_map/all_gather | solution.py:12
  131.5 60.8 %while.10 = (s32[]{:T(128)}, f32[2,128,128]{2,1,0:T(8,128)S(1)}, s32[]{:T(128)}, f32[64,2,128,128]{3,2,1,0:T(8,128)}, s32[]{:T(128)}, /*index=5*/s32[]{:T(128)}, s32[]{:T(128)}) while((s32[]{:T(128)}, f32[2,128,128]{2,1,0:T(8,128)S(1)}, s32[]{:T(128)}, f32[64,2,128,128]{3,2,1,0:T(8,128)}, s32[]{:T(128)}, /*index=5*/s32[]{:T(128)}, ...), condition=%wide.region_2.3_spmd, body=%wide.region_1.2_spmd.sunk | while | flops 32773 | bytes 393331 | solution.py:18
  131.5 0.9 bitcast_add_fusion.2
  132.4 0.9 bitcast_add_fusion.2
  133.4 0.9 bitcast_add_fusion.2
  134.4 0.9 bitcast_add_fusion.2
  135.3 0.9 bitcast_add_fusion.2
  136.3 0.9 bitcast_add_fusion.2
  137.3 0.9 bitcast_add_fusion.2
  142.1 0.9 bitcast_add_fusion.2
  144.0 0.9 bitcast_add_fusion.2
  160.4 0.9 bitcast_add_fusion.2
  162.3 0.9 bitcast_add_fusion.2
  178.7 0.9 bitcast_add_fusion.2
  180.7 0.9 bitcast_add_fusion.2
  192.2 1.1 subtract_add_fusion
  193.3 7.1 %all-to-all-start.1 = ((f32[8,2,128,128]{3,2,1,0:T(8,128)}), f32[8,2,128,128]{3,2,1,0:T(8,128)S(1)}, u32[]{:S(2)}, u32[]{:S(2)}) async-start(f32[8,2,128,128]{3,2,1,0:T(8,128)} %subtract_add_fusion), calls=%async_computation.1 | async-start | bytes 2097152 | tf_op jit(solution)/shard_map/all_to_all | solution.py:50
  200.4 29.4 %all-to-all-done.1 = f32[8,2,128,128]{3,2,1,0:T(8,128)S(1)} async-done(((f32[8,2,128,128]{3,2,1,0:T(8,128)}), f32[8,2,128,128]{3,2,1,0:T(8,128)S(1)}, u32[]{:S(2)}, u32[]{:S(2)}) %all-to-all-start.1) | async-done | bytes 1048608 | tf_op jit(solution)/shard_map/all_to_all | solution.py:50
  229.9 2.5 %convolution_bitcast_fusion.2 = f32[128,16,128]{0,2,1:T(8,128)S(1)} fusion(f32[16,128,128]{2,1,0:T(8,128)S(1)} %bitcast.55, bf16[128,2048]{1,0:T(8,128)(2,1)} %param.6), kind=kOutput, calls=%fused_computation.9 | convolution fusion | flops 404226048 | bytes 2621440 | tf_op jit(solution)/shard_map/dtu,tuj->dtj/dot_general | solution.py:59
  232.4 2.0 multiply_reduce_fusion
  234.8 1.0 copy.17
  (63 shorter events, 48.5 us)
Async XLA Ops:
  6.5 1.8 copy-start
  6.5 124.9 %all-gather.2.cloned.1.call-start = ((), (), s32[]{:S(2)}) async-start(), calls=%async_computation.2 | async-start | bytes 8519680 | tf_op jit(solution)/shard_map/all_gather | solution.py:12
  45.8 188.6 %copy-start.1 = (f32[2048]{0:T(1024)S(1)}, f32[2048]{0:T(1024)}, u32[]{:S(2)}) copy-start(f32[2048]{0:T(1024)} %param.9) | copy-start | bytes 24580
  193.3 36.5 %all-to-all-start.1 = ((f32[8,2,128,128]{3,2,1,0:T(8,128)}), f32[8,2,128,128]{3,2,1,0:T(8,128)S(1)}, u32[]{:S(2)}, u32[]{:S(2)}) async-start(f32[8,2,128,128]{3,2,1,0:T(8,128)} %subtract_add_fusion), calls=%async_computation.1 | async-start | bytes 2097152 | tf_op jit(solution)/shard_map/all_to_all | solution.py:50
Sparse Core Ops, SparseCore 0:
  47.6 83.8 all-gather.1
where the time goes:
time: 244 us; the launch traced here: 243 us
  waiting for transfers between devices  113 us (46%)
  other arithmetic  63 us (26%)
  blocking collectives  37.1 us (15%)
  between operations  13.5 us (6%)
  starting transfers between devices  7.13 us (3%)
  matrix products  4.83 us (2%)
    all_gather x1, waiting for transfers between devices, carried_in(): gathered = lax.all_gather(part, axis)  84 us
    add x63, other arithmetic, add_states(): return earlier + later  59 us
    all_to_all x1, blocking collectives, local(): lax.all_to_all(local_state[None], 'narrow', split_axis=1, concat_axis=0,...  37.1 us
    all_to_all x1, waiting for transfers between devices, local(): lax.all_to_all(block_prefix, 'narrow', split_axis=0, concat_axis=1, tiled...  29.4 us
    all_to_all x1, starting transfers between devices, local(): lax.all_to_all(block_prefix, 'narrow', split_axis=0, concat_axis=1, tiled...  7.12 us
  transfers between devices with their start and end apart: 2, of which 2 were waited for; matrix products, arithmetic and copies ran while one was open for 0% of the time, Pallas kernels for 0%

commit v1 on v0

v1 whole, which is shorter than its diff:
```python
import jax
import jax.numpy as jnp
from jax import lax
from jax.experimental import pallas as pl
from jax.experimental.pallas import tpu as pltpu
from jax.sharding import Mesh, PartitionSpec as P

H = 16
DK = 128
GROUP = ("x", "core", "z")
WHOLE = ("y", "x", "core", "z")
SIZES = (8, 4, 2, 8)


def feature(rows):
    wide = rows.astype(jnp.float32)
    grown = jnp.where(wide > 0.0, wide + 1.0, jnp.exp(jnp.minimum(wide, 0.0)))
    return grown.astype(jnp.bfloat16)


def state_kernel(keys_ref, values_ref, state_ref):
    for head in range(H):
        lanes = slice(head * DK, (head + 1) * DK)
        state_ref[head] = lax.dot_general(
            feature(keys_ref[:, lanes]),
            values_ref[:, lanes],
            (((0,), (0,)), ((), ())),
            preferred_element_type=jnp.float32,
        )


def scan_kernel(start_ref, parts_ref, prefix_ref):
    running = start_ref[...]
    for block in range(parts_ref.shape[0]):
        prefix_ref[block] = running
        running = running + parts_ref[block]


def attend_kernel(queries_ref, keys_ref, values_ref, gain_ref, prefix_ref, out_ref):
    rows = queries_ref.shape[0]
    at = lax.broadcasted_iota(jnp.int32, (rows, rows), 0)
    seen = lax.broadcasted_iota(jnp.int32, (rows, rows), 1)
    causal = seen <= at
    for head in range(H):
        lanes = slice(head * DK, (head + 1) * DK)
        fq = feature(queries_ref[:, lanes])
        fk = feature(keys_ref[:, lanes])
        scores = lax.dot_general(
            fq, fk, (((1,), (1,)), ((), ())), preferred_element_type=jnp.float32
        )
        weights = jnp.where(causal, scores, 0.0).astype(jnp.bfloat16)
        prefix = prefix_ref[head]
        high = prefix.astype(jnp.bfloat16)
        rest = prefix - high.astype(jnp.float32)
        middle = rest.astype(jnp.bfloat16)
        low = (rest - middle.astype(jnp.float32)).astype(jnp.bfloat16)
        left = jnp.concatenate([weights, fq, fq, fq], axis=1)
        right = jnp.concatenate([values_ref[:, lanes], high, middle, low], axis=0)
        mixed = jnp.dot(left, right, preferred_element_type=jnp.float32)
        meansq = jnp.mean(mixed * mixed, axis=-1, keepdims=True)
        scaled = gain_ref[:, lanes] * mixed * lax.rsqrt(meansq + 1e-05)
        out_ref[:, lanes] = scaled.astype(jnp.bfloat16)


def on_chip(kernel, shape, dtype, count):
    whole = pl.BlockSpec(memory_space=pltpu.VMEM)
    return pl.pallas_call(
        kernel,
        out_shape=jax.ShapeDtypeStruct(shape, dtype),
        in_specs=[whole] * count,
        out_specs=whole,
        compiler_params=pltpu.CompilerParams(vmem_limit_bytes=32 * 2**20),
    )


def local(queries, keys, values, norm_gain):
    rows = queries.shape[0]
    group = SIZES[1] * SIZES[2] * SIZES[3]
    piece = H * DK // group
    state = on_chip(state_kernel, (H, DK, DK), jnp.float32, 2)(keys, values)
    parts = lax.all_to_all(state.reshape(group, piece, DK), GROUP, 0, 0, tiled=True)
    total = jnp.sum(parts, axis=0)
    planes = lax.all_to_all(
        jnp.broadcast_to(total[None], (SIZES[0], piece, DK)), "y", 0, 0, tiled=True
    )
    before = jnp.arange(SIZES[0]) < lax.axis_index("y")
    start = jnp.sum(jnp.where(before[:, None, None], planes, 0.0), axis=0)
    prefix = on_chip(scan_kernel, parts.shape, jnp.float32, 2)(start, parts)
    prefix = lax.all_to_all(prefix, GROUP, 0, 0, tiled=True).reshape(H, DK, DK)
    return on_chip(attend_kernel, (rows, H * DK), jnp.bfloat16, 5)(
        queries, keys, values, norm_gain.reshape(1, H * DK), prefix
    )


def solution(mesh):
    mesh = Mesh(mesh.devices.reshape(SIZES), WHOLE)
    split = P(WHOLE, None)
    return jax.shard_map(
        local, mesh=mesh, in_specs=(split, split, split, P()), out_specs=split, check_vma=False
    )
```

time: 244 us -> 101 us (0.41)
  the two profiles are of different devices: /device:TPU:63 before, /device:TPU:1 now
where the time goes in v1:
time: 101 us
  blocking collectives  79 us (78%)
  waiting for transfers between devices  7.88 us (8%)
  starting transfers between devices  6.82 us (7%)
  Pallas kernels  4.07 us (4%)
  local copies, waits for them, and re-layouts  2.77 us (3%)
    all_to_all x1, blocking collectives, local(): lax.all_to_all(state.reshape(group, piece, DK), GROUP, 0, 0, tiled=True)  42.7 us
    all_to_all x1, blocking collectives, local(): prefix = lax.all_to_all(prefix, GROUP, 0, 0, tiled=True).reshape(H, DK, DK)  36.3 us
    all_to_all x1, waiting for transfers between devices, local(): lax.all_to_all(jnp.broadcast_to(total[None], (SIZES[0], piece, DK)), 'y',...  7.88 us
    all_to_all x1, starting transfers between devices, local(): lax.all_to_all(jnp.broadcast_to(total[None], (SIZES[0], piece, DK)), 'y',...  6.82 us
    pallas_call x1, Pallas kernels, local(): on_chip(attend_kernel, (rows, H * DK), jnp.bfloat16, 5)  3.5 us
    unnamed x12, local copies, waits for them, and re-layouts  2.11 us
  transfers between devices with their start and end apart: 1, of which 1 were waited for; matrix products, arithmetic and copies ran while one was open for 0% of the time, Pallas kernels for 0%

profile of v1, /device:TPU:1, one launch (start us, length us, event | category | flops | bytes accessed | tf_op | source)
XLA Modules:
  0.0 100.8 jit_solution(18166747923886417964)
XLA Ops:
  0.0 0.0 copy-start
  0.0 1.0 %copy-done = bf16[128,2048]{1,0:T(8,128)(2,1)S(1)} copy-done((bf16[128,2048]{1,0:T(8,128)(2,1)S(1)}, bf16[128,2048]{1,0:T(8,128)(2,1)}, u32[]{:S(2)}) %copy-start) | copy-done | bytes 524312
  1.0 0.0 copy-start.2
  1.0 1.0 %copy-done.2 = bf16[128,2048]{1,0:T(8,128)(2,1)S(1)} copy-done((bf16[128,2048]{1,0:T(8,128)(2,1)S(1)}, bf16[128,2048]{1,0:T(8,128)(2,1)}, u32[]{:S(2)}) %copy-start.2) | copy-done | bytes 524312
  2.1 0.5 shard_map.46
  2.6 42.7 %all_to_all.15.parts_ref = f32[64,32,128]{2,1,0:T(8,128)S(1)} all-to-all(f32[64,32,128]{2,1,0:T(8,128)S(1)} %bitcast.4), channel_id=1, replica_groups=mesh['y'=8,'x'=4,'core'=2,'z'=8] {'x','core','z'}, dimensions={0} | all-to-all | bytes 2097152 | tf_op jit(solution)/shard_map/all_to_all | solution.py:81
  45.3 0.1 reduce_sum.18
  45.4 0.7 broadcast_in_dim.20
  46.1 6.8 %all-to-all-start.1 = ((f32[8,32,128]{2,1,0:T(8,128)}), f32[8,32,128]{2,1,0:T(8,128)S(1)}, u32[]{:S(2)}, u32[]{:S(2)}) async-start(f32[8,32,128]{2,1,0:T(8,128)} %broadcast_in_dim.20), calls=%async_computation.1 | async-start | bytes 262144 | tf_op jit(solution)/shard_map/all_to_all | solution.py:83
  52.9 7.9 %all-to-all-done.1 = f32[8,32,128]{2,1,0:T(8,128)S(1)} async-done(((f32[8,32,128]{2,1,0:T(8,128)}), f32[8,32,128]{2,1,0:T(8,128)S(1)}, u32[]{:S(2)}, u32[]{:S(2)}) %all-to-all-start.1) | async-done | bytes 131104 | tf_op jit(solution)/shard_map/all_to_all | solution.py:83
  60.8 0.1 select_reduce_fusion.start_ref
  60.9 0.1 shard_map.47
  60.9 0.0 copy-start.1
  61.0 0.0 copy-start.3
  61.0 0.0 copy-start.4
  61.0 0.0 copy-start.5
  61.0 36.3 %all_to_all.16 = f32[64,32,128]{2,1,0:T(8,128)S(1)} all-to-all(f32[64,32,128]{2,1,0:T(8,128)S(1)} %shard_map.47), channel_id=1, replica_groups=mesh['y'=8,'x'=4,'core'=2,'z'=8] {'x','core','z'}, dimensions={0} | all-to-all | bytes 2097152 | tf_op jit(solution)/shard_map/all_to_all | solution.py:89
  97.3 0.0 copy-done.1
  97.3 0.0 copy-done.3
  97.3 0.0 copy-done.4
  97.3 0.0 copy-done.5
  97.3 3.5 %shard_map.48 = bf16[128,2048]{1,0:T(8,128)(2,1)} custom-call(bf16[128,2048]{1,0:T(8,128)(2,1)S(1)} %copy-done.4, bf16[128,2048]{1,0:T(8,128)(2,1)S(1)} %copy-done.1, bf16[128,2048]{1,0:T(8,128)(2,1)S(1)} %copy-done.3, f32[1,2048]{1,0:T(1,128)S(1)} %bitcast.5, f32[16,128,128]{2,1,0:T(8,128)S(1)} %bitcast.3), custom_call_target="tpu_custom_call" | custom-call | tf_op jit(solution)/shard_map/pallas_call | solution.py:90
  (1 shorter events, 0.0 us)
Async XLA Ops:
  0.0 1.0 %copy-start = (bf16[128,2048]{1,0:T(8,128)(2,1)S(1)}, bf16[128,2048]{1,0:T(8,128)(2,1)}, u32[]{:S(2)}) copy-start(bf16[128,2048]{1,0:T(8,128)(2,1)} %keys_ref.3) | copy-start | bytes 1572868
  1.0 1.0 %copy-start.2 = (bf16[128,2048]{1,0:T(8,128)(2,1)S(1)}, bf16[128,2048]{1,0:T(8,128)(2,1)}, u32[]{:S(2)}) copy-start(bf16[128,2048]{1,0:T(8,128)(2,1)} %values_ref.3) | copy-start | bytes 1572868
  46.1 14.7 %all-to-all-start.1 = ((f32[8,32,128]{2,1,0:T(8,128)}), f32[8,32,128]{2,1,0:T(8,128)S(1)}, u32[]{:S(2)}, u32[]{:S(2)}) async-start(f32[8,32,128]{2,1,0:T(8,128)} %broadcast_in_dim.20), calls=%async_computation.1 | async-start | bytes 262144 | tf_op jit(solution)/shard_map/all_to_all | solution.py:83
  60.9 36.4 %copy-start.1 = (bf16[128,2048]{1,0:T(8,128)(2,1)S(1)}, bf16[128,2048]{1,0:T(8,128)(2,1)}, u32[]{:S(2)}) copy-start(bf16[128,2048]{1,0:T(8,128)(2,1)} %keys_ref.3) | copy-start | bytes 1572868
  61.0 36.4 %copy-start.3 = (bf16[128,2048]{1,0:T(8,128)(2,1)S(1)}, bf16[128,2048]{1,0:T(8,128)(2,1)}, u32[]{:S(2)}) copy-start(bf16[128,2048]{1,0:T(8,128)(2,1)} %values_ref.3) | copy-start | bytes 1572868
  61.0 36.3 %copy-start.4 = (bf16[128,2048]{1,0:T(8,128)(2,1)S(1)}, bf16[128,2048]{1,0:T(8,128)(2,1)}, u32[]{:S(2)}) copy-start(bf16[128,2048]{1,0:T(8,128)(2,1)} %queries_ref.1) | copy-start | bytes 1572868
  61.0 36.3 %copy-start.5 = (f32[2048]{0:T(1024)S(1)}, f32[2048]{0:T(1024)}, u32[]{:S(2)}) copy-start(f32[2048]{0:T(1024)} %param.7) | copy-start | bytes 24580

commit v2 on v1

v2 whole, which is shorter than its diff:
```python
import itertools

import jax
import jax.numpy as jnp
from jax import lax
from jax.experimental import pallas as pl
from jax.experimental.pallas import tpu as pltpu
from jax.sharding import Mesh, PartitionSpec as P

H = 16
DK = 128
SIZES = (8, 4, 2, 8)
WHOLE = ("y", "x", "core", "z")
PLANE = ("z", "core", "x")
TOGETHER = 8
LOADS = 1
LIMIT = 16 * 2**20


def feature(rows):
    wide = rows.astype(jnp.float32)
    grown = jnp.where(wide > 0.0, wide + 1.0, jnp.exp(jnp.minimum(wide, 0.0)))
    return grown.astype(jnp.bfloat16)


def lanes_of(head):
    return slice(head * DK, (head + 1) * DK)


def state_kernel(keys_hbm, values_hbm, state_ref, keys_ref, values_ref, arrived):
    loads = []
    for number, (source, target) in enumerate(
        ((keys_hbm, keys_ref), (values_hbm, values_ref))
    ):
        for half in range(LOADS):
            rows = pl.ds(half * (target.shape[0] // LOADS), target.shape[0] // LOADS)
            load = pltpu.make_async_copy(
                source.at[rows], target.at[rows], arrived.at[number, half]
            )
            load.start()
            loads.append(load)
    for load in loads:
        load.wait()
    for head in range(H):
        state_ref[head] = lax.dot_general(
            feature(keys_ref[:, lanes_of(head)]),
            values_ref[:, lanes_of(head)],
            (((0,), (0,)), ((), ())),
            preferred_element_type=jnp.float32,
        )


def total_kernel(parts_ref, totals_ref):
    sums = [parts_ref[lane] for lane in range(4)]
    for block in range(4, parts_ref.shape[0]):
        sums[block % 4] = sums[block % 4] + parts_ref[block]
    total = (sums[0] + sums[1]) + (sums[2] + sums[3])
    for plane in range(totals_ref.shape[0]):
        totals_ref[plane] = total


def scan_kernel(planes_ref, parts_ref, prefix_ref):
    place = lax.axis_index("y")
    running = jnp.zeros_like(planes_ref[0])
    for plane in range(planes_ref.shape[0] - 1):
        running = running + jnp.where(plane < place, planes_ref[plane], 0.0)
    for x, core, z in itertools.product(*(range(size) for size in SIZES[1:])):
        block = (z * SIZES[2] + core) * SIZES[1] + x
        prefix_ref[block] = running
        running = running + parts_ref[block]


def attend_kernel(queries_ref, keys_ref, values_ref, gain_ref, prefix_ref, out_ref):
    rows = queries_ref.shape[0]
    at = lax.broadcasted_iota(jnp.int32, (rows, rows), 0)
    seen = lax.broadcasted_iota(jnp.int32, (rows, rows), 1)
    causal = seen <= at
    for first in range(0, H, TOGETHER):
        heads = range(first, first + TOGETHER)
        fq = [feature(queries_ref[:, lanes_of(head)]) for head in heads]
        fk = [feature(keys_ref[:, lanes_of(head)]) for head in heads]
        scores = [
            lax.dot_general(a, b, (((1,), (1,)), ((), ())), preferred_element_type=jnp.float32)
            for a, b in zip(fq, fk)
        ]
        weights = [jnp.where(causal, part, 0.0).astype(jnp.bfloat16) for part in scores]
        mixed = []
        for head, a, w in zip(heads, fq, weights):
            prefix = prefix_ref[head]
            high = prefix.astype(jnp.bfloat16)
            rest = prefix - high.astype(jnp.float32)
            middle = rest.astype(jnp.bfloat16)
            low = (rest - middle.astype(jnp.float32)).astype(jnp.bfloat16)
            mixed.append(
                jnp.dot(
                    jnp.concatenate([w, a, a, a], axis=1),
                    jnp.concatenate([values_ref[:, lanes_of(head)], high, middle, low], axis=0),
                    preferred_element_type=jnp.float32,
                )
            )
        for head, part in zip(heads, mixed):
            meansq = jnp.mean(part * part, axis=-1, keepdims=True)
            scaled = gain_ref[:, lanes_of(head)] * part * lax.rsqrt(meansq + 1e-05)
            out_ref[:, lanes_of(head)] = scaled.astype(jnp.bfloat16)


def on_chip(kernel, count, *results, flops=0):
    whole = pl.BlockSpec(memory_space=pltpu.VMEM)
    shapes = [jax.ShapeDtypeStruct(shape, dtype) for shape, dtype in results]
    return pl.pallas_call(
        kernel,
        out_shape=shapes,
        in_specs=[whole] * count,
        out_specs=[whole] * len(shapes),
        compiler_params=pltpu.CompilerParams(vmem_limit_bytes=12 * 2**20),
        cost_estimate=pl.CostEstimate(
            flops=flops, bytes_accessed=3 * 2**20, transcendentals=0
        ),
    )


def local(queries, keys, values, norm_gain):
    rows, width = queries.shape
    planes, group = SIZES[0], SIZES[1] * SIZES[2] * SIZES[3]
    piece = width // group
    f32 = jnp.float32
    flops = 2 * H * rows * DK * DK
    state = pl.pallas_call(
        state_kernel,
        out_shape=jax.ShapeDtypeStruct((H, DK, DK), f32),
        in_specs=[pl.BlockSpec(memory_space=pl.ANY)] * 2,
        out_specs=pl.BlockSpec(memory_space=pltpu.VMEM),
        scratch_shapes=[pltpu.VMEM((rows, width), jnp.bfloat16)] * 2
        + [pltpu.SemaphoreType.DMA((2, LOADS))],
        compiler_params=pltpu.CompilerParams(vmem_limit_bytes=LIMIT),
    )(*(pltpu.with_memory_space_constraint(part, pltpu.HBM) for part in (keys, values)))
    parts = lax.all_to_all(state.reshape(group, piece, DK), PLANE, 0, 0, tiled=True)
    [totals] = on_chip(total_kernel, 1, ((planes, piece, DK), f32))(parts)
    totals = lax.all_to_all(totals, "y", 0, 0, tiled=True)
    [prefix] = on_chip(scan_kernel, 2, (parts.shape, f32))(totals, parts)
    prefix = lax.all_to_all(prefix, PLANE, 0, 0, tiled=True).reshape(H, DK, DK)
    [out] = on_chip(attend_kernel, 5, ((rows, width), jnp.bfloat16), flops=7 * flops)(
        queries, keys, values, norm_gain.reshape(1, width), prefix
    )
    return out


def solution(mesh):
    mesh = Mesh(mesh.devices.reshape(SIZES), WHOLE)
    split = P(WHOLE, None)
    return jax.shard_map(
        local, mesh=mesh, in_specs=(split, split, split, P()), out_specs=split, check_vma=False
    )
```

time: 101 us -> 97.5 us (0.965)
  blocking collectives: 79 us -> 93 us
  waiting for transfers between devices: 7.88 us -> 0 us
  starting transfers between devices: 6.82 us -> 0 us
  local copies, waits for them, and re-layouts: 2.77 us -> 0.03 us
    all_to_all x2 -> x3, blocking collectives: 79 us -> 93 us  [the longest x1 42.4 us: local(): lax.all_to_all(state.reshape(group, piece, DK), PLANE, 0, 0, tiled=True)]
    all_to_all x1 -> x0, waiting for transfers between devices: 7.88 us -> none  [local(): lax.all_to_all(jnp.broadcast_to(total[None], (SIZES[0], piece, DK)), 'y',...]
    all_to_all x1 -> x0, starting transfers between devices: 6.82 us -> none  [local(): lax.all_to_all(jnp.broadcast_to(total[None], (SIZES[0], piece, DK)), 'y',...]
    unnamed x12 -> x8, local copies, waits for them, and re-layouts: 2.11 us -> 0.03 us
    pallas_call x3 -> x4, Pallas kernels: 4.07 us -> 4.07 us  [the longest x1 2.18 us: local(): on_chip(attend_kernel, 5, ((rows, width), jnp.bfloat16), flops=7 * flops)]
  transfers between devices with their start and end apart: 1 -> 0, of which waited for: 1 -> 0; matrix products, arithmetic and copies ran while one was open for 0% -> 0% of each run, Pallas kernels for 0% -> 0%
where the time goes in v2:
time: 97.5 us; the launch traced here: 97.1 us
  blocking collectives  93 us (95%)
  Pallas kernels  4.07 us (4%)
    all_to_all x1, blocking collectives, local(): lax.all_to_all(state.reshape(group, piece, DK), PLANE, 0, 0, tiled=True)  42.4 us
    all_to_all x1, blocking collectives, local(): prefix = lax.all_to_all(prefix, PLANE, 0, 0, tiled=True).reshape(H, DK, DK)  36 us
    all_to_all x1, blocking collectives, local(): totals = lax.all_to_all(totals, 'y', 0, 0, tiled=True)  14.6 us
    pallas_call x1, Pallas kernels, local(): on_chip(attend_kernel, 5, ((rows, width), jnp.bfloat16), flops=7 * flops)  2.18 us

profile of v2, /device:TPU:1, one launch (start us, length us, event | category | flops | bytes accessed | tf_op | source)
XLA Modules:
  0.0 97.1 jit_solution(6426537928295896936)
XLA Ops:
  0.0 1.7 %shard_map.46 = f32[16,128,128]{2,1,0:T(8,128)S(1)} custom-call(bf16[128,2048]{1,0:T(8,128)(2,1)} %keys_ref.1, bf16[128,2048]{1,0:T(8,128)(2,1)} %values_ref.1), custom_call_target="tpu_custom_call" | custom-call | tf_op jit(solution)/shard_map/pallas_call | solution.py:128
  1.7 42.4 %all_to_all.15.parts_ref = f32[64,32,128]{2,1,0:T(8,128)S(1)} all-to-all(f32[64,32,128]{2,1,0:T(8,128)S(1)} %bitcast.4), channel_id=1, replica_groups=mesh['y'=8,'x'=4,'core'=2,'z'=8] {'z','core','x'}, dimensions={0} | all-to-all | bytes 2097152 | tf_op jit(solution)/shard_map/all_to_all | solution.py:137
  44.1 0.1 shard_map.47
  44.2 14.6 %all_to_all.16.planes_ref = f32[8,32,128]{2,1,0:T(8,128)S(1)} all-to-all(f32[8,32,128]{2,1,0:T(8,128)S(1)} %shard_map.47), channel_id=1, replica_groups=mesh['y'=8,'x'=4,'core'=2,'z'=8] {'y'}, dimensions={0} | all-to-all | bytes 262144 | tf_op jit(solution)/shard_map/all_to_all | solution.py:139
  58.8 0.1 shard_map.48
  58.9 0.0 copy-start
  58.9 0.0 copy-start.1
  58.9 0.0 copy-start.2
  58.9 0.0 copy-start.3
  58.9 36.0 %all_to_all.17 = f32[64,32,128]{2,1,0:T(8,128)S(1)} all-to-all(f32[64,32,128]{2,1,0:T(8,128)S(1)} %shard_map.48), channel_id=1, replica_groups=mesh['y'=8,'x'=4,'core'=2,'z'=8] {'z','core','x'}, dimensions={0} | all-to-all | bytes 2097152 | tf_op jit(solution)/shard_map/all_to_all | solution.py:141
  94.9 0.0 copy-done
  94.9 0.0 copy-done.1
  94.9 0.0 copy-done.2
  94.9 0.0 copy-done.3
  95.0 2.2 %shard_map.49 = bf16[128,2048]{1,0:T(8,128)(2,1)} custom-call(bf16[128,2048]{1,0:T(8,128)(2,1)S(1)} %copy-done.2, bf16[128,2048]{1,0:T(8,128)(2,1)S(1)} %copy-done, bf16[128,2048]{1,0:T(8,128)(2,1)S(1)} %copy-done.1, f32[1,2048]{1,0:T(1,128)S(1)} %bitcast.5, f32[16,128,128]{2,1,0:T(8,128)S(1)} %bitcast.3), custom_call_target="tpu_custom_call" | custom-call | flops 469762048 | bytes 3145728 | tf_op jit(solution)/shard_map/pallas_call | solution.py:142
Async XLA Ops:
  58.9 36.1 %copy-start = (bf16[128,2048]{1,0:T(8,128)(2,1)S(1)}, bf16[128,2048]{1,0:T(8,128)(2,1)}, u32[]{:S(2)}) copy-start(bf16[128,2048]{1,0:T(8,128)(2,1)} %keys_ref.1) | copy-start | bytes 1572868
  58.9 36.1 %copy-start.1 = (bf16[128,2048]{1,0:T(8,128)(2,1)S(1)}, bf16[128,2048]{1,0:T(8,128)(2,1)}, u32[]{:S(2)}) copy-start(bf16[128,2048]{1,0:T(8,128)(2,1)} %values_ref.1) | copy-start | bytes 1572868
  58.9 36.1 %copy-start.2 = (bf16[128,2048]{1,0:T(8,128)(2,1)S(1)}, bf16[128,2048]{1,0:T(8,128)(2,1)}, u32[]{:S(2)}) copy-start(bf16[128,2048]{1,0:T(8,128)(2,1)} %queries_ref.1) | copy-start | bytes 1572868
  58.9 36.1 %copy-start.3 = (f32[2048]{0:T(1024)S(1)}, f32[2048]{0:T(1024)}, u32[]{:S(2)}) copy-start(f32[2048]{0:T(1024)} %param.7) | copy-start | bytes 24580

commit v3 on v2

v3 whole, which is shorter than its diff:
```python
import itertools

import jax
import jax.numpy as jnp
from jax import lax
from jax.experimental import pallas as pl
from jax.experimental.pallas import tpu as pltpu
from jax.sharding import Mesh, PartitionSpec as P

H = 16
DK = 128
SIZES = (8, 4, 2, 8)
WHOLE = ("y", "x", "core", "z")
PLANE = ("z", "core", "x")
TOGETHER = 8
LIMIT = 16 * 2**20


def feature(rows):
    wide = rows.astype(jnp.float32)
    grown = jnp.where(wide > 0.0, wide + 1.0, jnp.exp(jnp.minimum(wide, 0.0)))
    return grown.astype(jnp.bfloat16)


def lanes_of(head):
    return slice(head * DK, (head + 1) * DK)


def scores_of(fq, fk, causal):
    scores = lax.dot_general(
        fq, fk, (((1,), (1,)), ((), ())), preferred_element_type=jnp.float32
    )
    return jnp.where(causal, scores, 0.0).astype(jnp.bfloat16)


def mask_of(rows):
    at = lax.broadcasted_iota(jnp.int32, (rows, rows), 0)
    return lax.broadcasted_iota(jnp.int32, (rows, rows), 1) <= at


def in_three(prefix):
    high = prefix.astype(jnp.bfloat16)
    rest = prefix - high.astype(jnp.float32)
    middle = rest.astype(jnp.bfloat16)
    return [high, middle, (rest - middle.astype(jnp.float32)).astype(jnp.bfloat16)]


def normed(mixed, gain):
    meansq = jnp.mean(mixed * mixed, axis=-1, keepdims=True)
    return (gain * mixed * lax.rsqrt(meansq + 1e-05)).astype(jnp.bfloat16)


def waits_first():
    return lax.axis_index("z") < SIZES[3] // 2


def state_kernel(
    keys_hbm,
    values_hbm,
    queries_hbm,
    state_ref,
    inner_ref,
    features_ref,
    keys_ref,
    values_ref,
    queries_ref,
    arrived,
):
    loads = [
        pltpu.make_async_copy(source, target, arrived.at[number])
        for number, (source, target) in enumerate(
            (
                (keys_hbm, keys_ref),
                (values_hbm, values_ref),
                (queries_hbm, queries_ref),
            )
        )
    ]
    for load in loads[:2]:
        load.start()
    for load in loads[:2]:
        load.wait()
    for head in range(H):
        state_ref[head] = lax.dot_general(
            feature(keys_ref[:, lanes_of(head)]),
            values_ref[:, lanes_of(head)],
            (((0,), (0,)), ((), ())),
            preferred_element_type=jnp.float32,
        )
    @pl.when(waits_first())
    def _():
        loads[2].start()
        loads[2].wait()
        causal = mask_of(queries_ref.shape[0])
        for first in range(0, H, TOGETHER):
            lanes = [lanes_of(head) for head in range(first, first + TOGETHER)]
            fq = [feature(queries_ref[:, part]) for part in lanes]
            fk = [feature(keys_ref[:, part]) for part in lanes]
            weights = [scores_of(a, b, causal) for a, b in zip(fq, fk)]
            for part, a, w in zip(lanes, fq, weights):
                inner_ref[:, part] = jnp.dot(
                    w, values_ref[:, part], preferred_element_type=jnp.float32
                )
                features_ref[:, part] = a


def total_kernel(parts_ref, totals_ref):
    sums = [parts_ref[lane] for lane in range(4)]
    for block in range(4, parts_ref.shape[0]):
        sums[block % 4] = sums[block % 4] + parts_ref[block]
    total = (sums[0] + sums[1]) + (sums[2] + sums[3])
    for plane in range(totals_ref.shape[0]):
        totals_ref[plane] = total


def scan_kernel(planes_ref, parts_ref, prefix_ref):
    place = lax.axis_index("y")
    running = jnp.zeros_like(planes_ref[0])
    for plane in range(planes_ref.shape[0] - 1):
        running = running + jnp.where(plane < place, planes_ref[plane], 0.0)
    for x, core, z in itertools.product(*(range(size) for size in SIZES[1:])):
        block = (z * SIZES[2] + core) * SIZES[1] + x
        prefix_ref[block] = running
        running = running + parts_ref[block]


def attend_kernel(
    queries_ref,
    keys_ref,
    values_ref,
    gain_ref,
    prefix_ref,
    inner_ref,
    features_ref,
    out_hbm,
    out_ref,
    left,
):
    def store(first):
        done = pl.ds(first * DK, TOGETHER * DK)
        return pltpu.make_async_copy(
            out_ref.at[:, done], out_hbm.at[:, done], left.at[first // TOGETHER]
        )

    @pl.when(waits_first())
    def _():
        for first in range(0, H, TOGETHER):
            for head in range(first, first + TOGETHER):
                lanes = lanes_of(head)
                fq = features_ref[:, lanes]
                outer = jnp.dot(
                    jnp.concatenate([fq] * 3, axis=1),
                    jnp.concatenate(in_three(prefix_ref[head]), axis=0),
                    preferred_element_type=jnp.float32,
                )
                out_ref[:, lanes] = normed(inner_ref[:, lanes] + outer, gain_ref[:, lanes])
            store(first).start()

    @pl.when(jnp.logical_not(waits_first()))
    def _():
        causal = mask_of(queries_ref.shape[0])
        for first in range(0, H, TOGETHER):
            heads = range(first, first + TOGETHER)
            fq = [feature(queries_ref[:, lanes_of(head)]) for head in heads]
            fk = [feature(keys_ref[:, lanes_of(head)]) for head in heads]
            weights = [scores_of(a, b, causal) for a, b in zip(fq, fk)]
            mixed = []
            for head, a, w in zip(heads, fq, weights):
                right = [values_ref[:, lanes_of(head)], *in_three(prefix_ref[head])]
                mixed.append(
                    jnp.dot(
                        jnp.concatenate([w, a, a, a], axis=1),
                        jnp.concatenate(right, axis=0),
                        preferred_element_type=jnp.float32,
                    )
                )
            for head, part in zip(heads, mixed):
                out_ref[:, lanes_of(head)] = normed(part, gain_ref[:, lanes_of(head)])
            store(first).start()

    for first in range(0, H, TOGETHER):
        store(first).wait()


def on_chip(kernel, count, *results, flops=0):
    whole = pl.BlockSpec(memory_space=pltpu.VMEM)
    shapes = [jax.ShapeDtypeStruct(shape, dtype) for shape, dtype in results]
    return pl.pallas_call(
        kernel,
        out_shape=shapes,
        in_specs=[whole] * count,
        out_specs=[whole] * len(shapes),
        compiler_params=pltpu.CompilerParams(vmem_limit_bytes=12 * 2**20),
        cost_estimate=pl.CostEstimate(
            flops=flops, bytes_accessed=3 * 2**20, transcendentals=0
        ),
    )


def local(queries, keys, values, norm_gain):
    rows, width = queries.shape
    planes, group = SIZES[0], SIZES[1] * SIZES[2] * SIZES[3]
    piece = width // group
    f32 = jnp.float32
    flops = 2 * H * rows * DK * DK
    state, inner, features = pl.pallas_call(
        state_kernel,
        out_shape=[
            jax.ShapeDtypeStruct((H, DK, DK), f32),
            jax.ShapeDtypeStruct((rows, width), f32),
            jax.ShapeDtypeStruct((rows, width), jnp.bfloat16),
        ],
        in_specs=[pl.BlockSpec(memory_space=pl.ANY)] * 3,
        out_specs=[pl.BlockSpec(memory_space=pltpu.VMEM)] * 3,
        scratch_shapes=[pltpu.VMEM((rows, width), jnp.bfloat16)] * 3
        + [pltpu.SemaphoreType.DMA((3,))],
        compiler_params=pltpu.CompilerParams(vmem_limit_bytes=LIMIT),
    )(*(pltpu.with_memory_space_constraint(part, pltpu.HBM) for part in (keys, values, queries)))
    parts = lax.all_to_all(state.reshape(group, piece, DK), PLANE, 0, 0, tiled=True)
    [totals] = on_chip(total_kernel, 1, ((planes, piece, DK), f32))(parts)
    totals = lax.all_to_all(totals, "y", 0, 0, tiled=True)
    [prefix] = on_chip(scan_kernel, 2, (parts.shape, f32))(totals, parts)
    prefix = lax.all_to_all(prefix, PLANE, 0, 0, tiled=True).reshape(H, DK, DK)
    return pl.pallas_call(
        attend_kernel,
        out_shape=jax.ShapeDtypeStruct((rows, width), jnp.bfloat16),
        in_specs=[pl.BlockSpec(memory_space=pltpu.VMEM)] * 7,
        out_specs=pl.BlockSpec(memory_space=pl.ANY),
        scratch_shapes=[
            pltpu.VMEM((rows, width), jnp.bfloat16),
            pltpu.SemaphoreType.DMA((H // TOGETHER,)),
        ],
        compiler_params=pltpu.CompilerParams(vmem_limit_bytes=LIMIT),
    )(queries, keys, values, norm_gain.reshape(1, width), prefix, inner, features)


def solution(mesh):
    mesh = Mesh(mesh.devices.reshape(SIZES), WHOLE)
    split = P(WHOLE, None)
    return jax.shard_map(
        local, mesh=mesh, in_specs=(split, split, split, P()), out_specs=split, check_vma=False
    )
```

time: 97.5 us -> 96.8 us (level)
  blocking collectives: 93 us -> 91.1 us
  Pallas kernels: 4.07 us -> 5.24 us
    all_to_all x1, blocking collectives: 42.4 us -> 40.5 us  [local(): lax.all_to_all(state.reshape(group, piece, DK), PLANE, 0, 0, tiled=True)]
    pallas_call x2, Pallas kernels: 3.9 us -> 5.07 us  [the longest x1 3.61 us: local(): pl.pallas_call(state_kernel, out_shape=[jax.ShapeDtypeStruct((H, DK, DK),...]
where the time goes in v3:
time: 96.8 us; the launch traced here: 96.4 us
  blocking collectives  91.1 us (94%)
  Pallas kernels  5.24 us (5%)
    all_to_all x1, blocking collectives, local(): lax.all_to_all(state.reshape(group, piece, DK), PLANE, 0, 0, tiled=True)  40.5 us
    all_to_all x1, blocking collectives, local(): prefix = lax.all_to_all(prefix, PLANE, 0, 0, tiled=True).reshape(H, DK, DK)  36 us
    all_to_all x1, blocking collectives, local(): totals = lax.all_to_all(totals, 'y', 0, 0, tiled=True)  14.6 us
    pallas_call x1, Pallas kernels, local(): pl.pallas_call(state_kernel, out_shape=[jax.ShapeDtypeStruct((H, DK, DK),...  3.61 us

profile of v3, /device:TPU:1, one launch (start us, length us, event | category | flops | bytes accessed | tf_op | source)
XLA Modules:
  0.0 96.4 jit_solution(15953596745036620476)
XLA Ops:
  0.0 3.6 %shard_map.46 = (f32[16,128,128]{2,1,0:T(8,128)S(1)}, f32[128,2048]{1,0:T(8,128)S(1)}, bf16[128,2048]{1,0:T(8,128)(2,1)S(1)}) custom-call(bf16[128,2048]{1,0:T(8,128)(2,1)} %keys_ref.1, bf16[128,2048]{1,0:T(8,128)(2,1)} %values_ref.1, bf16[128,2048]{1,0:T(8,128)(2,1)} %queries_ref.1), custom_call_target="tpu_custom_call" | custom-call | tf_op jit(solution)/shard_map/pallas_call | solution.py:206
  3.6 40.5 %all_to_all.15.parts_ref = f32[64,32,128]{2,1,0:T(8,128)S(1)} all-to-all(f32[64,32,128]{2,1,0:T(8,128)S(1)} %bitcast.4), channel_id=1, replica_groups=mesh['y'=8,'x'=4,'core'=2,'z'=8] {'z','core','x'}, dimensions={0} | all-to-all | bytes 2097152 | tf_op jit(solution)/shard_map/all_to_all | solution.py:219
  44.1 0.1 shard_map.47
  44.2 14.6 %all_to_all.16.planes_ref = f32[8,32,128]{2,1,0:T(8,128)S(1)} all-to-all(f32[8,32,128]{2,1,0:T(8,128)S(1)} %shard_map.47), channel_id=1, replica_groups=mesh['y'=8,'x'=4,'core'=2,'z'=8] {'y'}, dimensions={0} | all-to-all | bytes 262144 | tf_op jit(solution)/shard_map/all_to_all | solution.py:221
  58.8 0.1 shard_map.48
  58.9 0.0 copy-start
  58.9 0.0 copy-start.1
  58.9 0.0 copy-start.2
  58.9 0.0 copy-start.3
  58.9 36.0 %all_to_all.17 = f32[64,32,128]{2,1,0:T(8,128)S(1)} all-to-all(f32[64,32,128]{2,1,0:T(8,128)S(1)} %shard_map.48), channel_id=1, replica_groups=mesh['y'=8,'x'=4,'core'=2,'z'=8] {'z','core','x'}, dimensions={0} | all-to-all | bytes 2097152 | tf_op jit(solution)/shard_map/all_to_all | solution.py:223
  94.9 0.0 copy-done
  94.9 0.0 copy-done.1
  94.9 0.0 copy-done.2
  95.0 0.0 copy-done.3
  95.0 1.5 %shard_map.49 = bf16[128,2048]{1,0:T(8,128)(2,1)} custom-call(bf16[128,2048]{1,0:T(8,128)(2,1)S(1)} %copy-done, bf16[128,2048]{1,0:T(8,128)(2,1)S(1)} %copy-done.1, bf16[128,2048]{1,0:T(8,128)(2,1)S(1)} %copy-done.2, f32[1,2048]{1,0:T(1,128)S(1)} %bitcast.5, f32[16,128,128]{2,1,0:T(8,128)S(1)} %bitcast.3, f32[128,2048]{1,0:T(8,128)S(1)} %get-tuple-element.9.inner_ref, ...), custom_call_target="tpu_custom_call" | custom-call | tf_op jit(solution)/shard_map/pallas_call | solution.py:224
Async XLA Ops:
  58.9 36.1 %copy-start = (bf16[128,2048]{1,0:T(8,128)(2,1)S(1)}, bf16[128,2048]{1,0:T(8,128)(2,1)}, u32[]{:S(2)}) copy-start(bf16[128,2048]{1,0:T(8,128)(2,1)} %queries_ref.1) | copy-start | bytes 1572868
  58.9 36.1 %copy-start.1 = (bf16[128,2048]{1,0:T(8,128)(2,1)S(1)}, bf16[128,2048]{1,0:T(8,128)(2,1)}, u32[]{:S(2)}) copy-start(bf16[128,2048]{1,0:T(8,128)(2,1)} %keys_ref.1) | copy-start | bytes 1572868
  58.9 36.1 %copy-start.2 = (bf16[128,2048]{1,0:T(8,128)(2,1)S(1)}, bf16[128,2048]{1,0:T(8,128)(2,1)}, u32[]{:S(2)}) copy-start(bf16[128,2048]{1,0:T(8,128)(2,1)} %values_ref.1) | copy-start | bytes 1572868
  58.9 36.1 %copy-start.3 = (f32[2048]{0:T(1024)S(1)}, f32[2048]{0:T(1024)}, u32[]{:S(2)}) copy-start(f32[2048]{0:T(1024)} %param.7) | copy-start | bytes 24580

commit v4 on v3

--- a/solution.py
+++ b/solution.py
@@ -10,8 +10,20 @@
 H = 16
 DK = 128
 SIZES = (8, 4, 2, 8)
-WHOLE = ("y", "x", "core", "z")
-PLANE = ("z", "core", "x")
+BITS = {"y": ("y2", "y1", "y0"), "x": ("x1", "x0"), "core": ("core",), "z": ("z2", "z1", "z0")}
+WHOLE = tuple(bit for axis in BITS.values() for bit in axis)
+ROWS = ("y0", "y1", "y2")
+PLANE = ("z2", "z1", "z0", "core", "x1", "x0")
+
+
+def index_in(order, **place):
+    index = 0
+    for bit in order:
+        axis = bit.rstrip("012")
+        index = 2 * index + (place[axis] >> int(bit[len(axis) :] or 0)) % 2
+    return index
+
+
 TOGETHER = 8
 LIMIT = 16 * 2**20
 
@@ -51,7 +63,7 @@
 
 
 def waits_first():
-    return lax.axis_index("z") < SIZES[3] // 2
+    return lax.axis_index(BITS["z"]) < SIZES[3] // 2
 
 
 def state_kernel(
@@ -114,12 +126,12 @@
 
 
 def scan_kernel(planes_ref, parts_ref, prefix_ref):
-    place = lax.axis_index("y")
+    place = lax.axis_index(BITS["y"])
     running = jnp.zeros_like(planes_ref[0])
     for plane in range(planes_ref.shape[0] - 1):
-        running = running + jnp.where(plane < place, planes_ref[plane], 0.0)
+        running = running + jnp.where(plane < place, planes_ref[index_in(ROWS, y=plane)], 0.0)
     for x, core, z in itertools.product(*(range(size) for size in SIZES[1:])):
-        block = (z * SIZES[2] + core) * SIZES[1] + x
+        block = index_in(PLANE, x=x, core=core, z=z)
         prefix_ref[block] = running
         running = running + parts_ref[block]
 
@@ -218,7 +230,7 @@
     )(*(pltpu.with_memory_space_constraint(part, pltpu.HBM) for part in (keys, values, queries)))
     parts = lax.all_to_all(state.reshape(group, piece, DK), PLANE, 0, 0, tiled=True)
     [totals] = on_chip(total_kernel, 1, ((planes, piece, DK), f32))(parts)
-    totals = lax.all_to_all(totals, "y", 0, 0, tiled=True)
+    totals = lax.all_to_all(totals, ROWS, 0, 0, tiled=True)
     [prefix] = on_chip(scan_kernel, 2, (parts.shape, f32))(totals, parts)
     prefix = lax.all_to_all(prefix, PLANE, 0, 0, tiled=True).reshape(H, DK, DK)
     return pl.pallas_call(
@@ -235,7 +247,7 @@
 
 
 def solution(mesh):
-    mesh = Mesh(mesh.devices.reshape(SIZES), WHOLE)
+    mesh = Mesh(mesh.devices.reshape((2,) * len(WHOLE)), WHOLE)
     split = P(WHOLE, None)
     return jax.shard_map(
         local, mesh=mesh, in_specs=(split, split, split, P()), out_specs=split, check_vma=False

time: 96.8 us -> 95.3 us (0.985)
  blocking collectives: 91.1 us -> 89.6 us
    all_to_all x1, blocking collectives: 14.6 us -> 13.4 us  [local(): totals = lax.all_to_all(totals, ROWS, 0, 0, tiled=True)]
where the time goes in v4:
time: 95.3 us; the launch traced here: 94.9 us
  blocking collectives  89.6 us (94%)
  Pallas kernels  5.24 us (5%)
    all_to_all x1, blocking collectives, local(): lax.all_to_all(state.reshape(group, piece, DK), PLANE, 0, 0, tiled=True)  40.5 us
    all_to_all x1, blocking collectives, local(): prefix = lax.all_to_all(prefix, PLANE, 0, 0, tiled=True).reshape(H, DK, DK)  35.7 us
    all_to_all x1, blocking collectives, local(): totals = lax.all_to_all(totals, ROWS, 0, 0, tiled=True)  13.4 us
    pallas_call x1, Pallas kernels, local(): pl.pallas_call(state_kernel, out_shape=[jax.ShapeDtypeStruct((H, DK, DK),...  3.61 us

profile of v4, /device:TPU:1, one launch (start us, length us, event | category | flops | bytes accessed | tf_op | source)
XLA Modules:
  0.0 94.9 jit_solution(5078765763807418336)
XLA Ops:
  0.0 3.6 %shard_map.46 = (f32[16,128,128]{2,1,0:T(8,128)S(1)}, f32[128,2048]{1,0:T(8,128)S(1)}, bf16[128,2048]{1,0:T(8,128)(2,1)S(1)}) custom-call(bf16[128,2048]{1,0:T(8,128)(2,1)} %keys_ref.1, bf16[128,2048]{1,0:T(8,128)(2,1)} %values_ref.1, bf16[128,2048]{1,0:T(8,128)(2,1)} %queries_ref.1), custom_call_target="tpu_custom_call" | custom-call | tf_op jit(solution)/shard_map/pallas_call | solution.py:218
  3.6 40.5 %all_to_all.15.parts_ref = f32[64,32,128]{2,1,0:T(8,128)S(1)} all-to-all(f32[64,32,128]{2,1,0:T(8,128)S(1)} %bitcast.4), channel_id=1, replica_groups=mesh['y2'=2,'y1'=2,'y0'=2,'x1'=2,'x0'=2,'core'=2,'z2'=2,'z1'=2,'z0'=2] {..., dimensions={0} | all-to-all | bytes 2097152 | tf_op jit(solution)/shard_map/all_to_all | solution.py:231
  44.1 0.1 shard_map.47
  44.2 13.4 %all_to_all.16.planes_ref = f32[8,32,128]{2,1,0:T(8,128)S(1)} all-to-all(f32[8,32,128]{2,1,0:T(8,128)S(1)} %shard_map.47), channel_id=1, replica_groups=mesh['y2'=2,'y1'=2,'y0'=2,'x1'=2,'x0'=2,'core'=2,'z2'=2,'z1'=2,'z0'=2] {..., dimensions={0} | all-to-all | bytes 262144 | tf_op jit(solution)/shard_map/all_to_all | solution.py:233
  57.6 0.1 shard_map.48
  57.7 0.0 copy-start
  57.7 0.0 copy-start.1
  57.7 0.0 copy-start.2
  57.7 0.0 copy-start.3
  57.8 35.7 %all_to_all.17 = f32[64,32,128]{2,1,0:T(8,128)S(1)} all-to-all(f32[64,32,128]{2,1,0:T(8,128)S(1)} %shard_map.48), channel_id=1, replica_groups=mesh['y2'=2,'y1'=2,'y0'=2,'x1'=2,'x0'=2,'core'=2,'z2'=2,'z1'=2,'z0'=2] {..., dimensions={0} | all-to-all | bytes 2097152 | tf_op jit(solution)/shard_map/all_to_all | solution.py:235
  93.4 0.0 copy-done
  93.4 0.0 copy-done.1
  93.4 0.0 copy-done.2
  93.4 0.0 copy-done.3
  93.4 1.5 %shard_map.49 = bf16[128,2048]{1,0:T(8,128)(2,1)} custom-call(bf16[128,2048]{1,0:T(8,128)(2,1)S(1)} %copy-done, bf16[128,2048]{1,0:T(8,128)(2,1)S(1)} %copy-done.1, bf16[128,2048]{1,0:T(8,128)(2,1)S(1)} %copy-done.2, f32[1,2048]{1,0:T(1,128)S(1)} %bitcast.5, f32[16,128,128]{2,1,0:T(8,128)S(1)} %bitcast.3, f32[128,2048]{1,0:T(8,128)S(1)} %get-tuple-element.9.inner_ref, ...), custom_call_target="tpu_custom_call" | custom-call | tf_op jit(solution)/shard_map/pallas_call | solution.py:236
Async XLA Ops:
  57.7 35.7 %copy-start = (bf16[128,2048]{1,0:T(8,128)(2,1)S(1)}, bf16[128,2048]{1,0:T(8,128)(2,1)}, u32[]{:S(2)}) copy-start(bf16[128,2048]{1,0:T(8,128)(2,1)} %queries_ref.1) | copy-start | bytes 1572868
  57.7 35.7 %copy-start.1 = (bf16[128,2048]{1,0:T(8,128)(2,1)S(1)}, bf16[128,2048]{1,0:T(8,128)(2,1)}, u32[]{:S(2)}) copy-start(bf16[128,2048]{1,0:T(8,128)(2,1)} %keys_ref.1) | copy-start | bytes 1572868
  57.7 35.7 %copy-start.2 = (bf16[128,2048]{1,0:T(8,128)(2,1)S(1)}, bf16[128,2048]{1,0:T(8,128)(2,1)}, u32[]{:S(2)}) copy-start(bf16[128,2048]{1,0:T(8,128)(2,1)} %values_ref.1) | copy-start | bytes 1572868
  57.7 35.7 %copy-start.3 = (f32[2048]{0:T(1024)S(1)}, f32[2048]{0:T(1024)}, u32[]{:S(2)}) copy-start(f32[2048]{0:T(1024)} %param.7) | copy-start | bytes 24580

commit v5 on v4

--- a/solution.py
+++ b/solution.py
@@ -78,31 +78,39 @@
     queries_ref,
     arrived,
 ):
-    loads = [
-        pltpu.make_async_copy(source, target, arrived.at[number])
-        for number, (source, target) in enumerate(
-            (
-                (keys_hbm, keys_ref),
-                (values_hbm, values_ref),
-                (queries_hbm, queries_ref),
+    def load(number, half):
+        source, target = (
+            (keys_hbm, keys_ref),
+            (values_hbm, values_ref),
+            (queries_hbm, queries_ref),
+        )[number]
+        rows = pl.ds(half * (target.shape[0] // 2), target.shape[0] // 2)
+        return pltpu.make_async_copy(
+            source.at[rows], target.at[rows], arrived.at[number, half]
+        )
+
+    for half in range(2):
+        for number in range(2):
+            load(number, half).start()
+    for half in range(2):
+        rows = slice(half * (keys_ref.shape[0] // 2), (half + 1) * (keys_ref.shape[0] // 2))
+        for number in range(2):
+            load(number, half).wait()
+        for head in range(H):
+            part = lax.dot_general(
+                feature(keys_ref[rows, lanes_of(head)]),
+                values_ref[rows, lanes_of(head)],
+                (((0,), (0,)), ((), ())),
+                preferred_element_type=jnp.float32,
             )
-        )
-    ]
-    for load in loads[:2]:
-        load.start()
-    for load in loads[:2]:
-        load.wait()
-    for head in range(H):
-        state_ref[head] = lax.dot_general(
-            feature(keys_ref[:, lanes_of(head)]),
-            values_ref[:, lanes_of(head)],
-            (((0,), (0,)), ((), ())),
-            preferred_element_type=jnp.float32,
-        )
+            state_ref[head] = part if half == 0 else state_ref[head] + part
+
     @pl.when(waits_first())
     def _():
-        loads[2].start()
-        loads[2].wait()
+        for half in range(2):
+            load(2, half).start()
+        for half in range(2):
+            load(2, half).wait()
         causal = mask_of(queries_ref.shape[0])
         for first in range(0, H, TOGETHER):
             lanes = [lanes_of(head) for head in range(first, first + TOGETHER)]
@@ -225,7 +233,7 @@
         in_specs=[pl.BlockSpec(memory_space=pl.ANY)] * 3,
         out_specs=[pl.BlockSpec(memory_space=pltpu.VMEM)] * 3,
         scratch_shapes=[pltpu.VMEM((rows, width), jnp.bfloat16)] * 3
-        + [pltpu.SemaphoreType.DMA((3,))],
+        + [pltpu.SemaphoreType.DMA((3, 2))],
         compiler_params=pltpu.CompilerParams(vmem_limit_bytes=LIMIT),
     )(*(pltpu.with_memory_space_constraint(part, pltpu.HBM) for part in (keys, values, queries)))
     parts = lax.all_to_all(state.reshape(group, piece, DK), PLANE, 0, 0, tiled=True)

time: 95.3 us -> 95.2 us (level)
  no operation moved by 1% of the time
where the time goes in v5:
time: 95.2 us; the launch traced here: 94.8 us
  blocking collectives  89.6 us (94%)
  Pallas kernels  5.16 us (5%)
    all_to_all x1, blocking collectives, local(): lax.all_to_all(state.reshape(group, piece, DK), PLANE, 0, 0, tiled=True)  40.5 us
    all_to_all x1, blocking collectives, local(): prefix = lax.all_to_all(prefix, PLANE, 0, 0, tiled=True).reshape(H, DK, DK)  35.7 us
    all_to_all x1, blocking collectives, local(): totals = lax.all_to_all(totals, ROWS, 0, 0, tiled=True)  13.4 us
    pallas_call x1, Pallas kernels, local(): pl.pallas_call(state_kernel, out_shape=[jax.ShapeDtypeStruct((H, DK, DK),...  3.53 us

profile of v5, /device:TPU:1, one launch (start us, length us, event | category | flops | bytes accessed | tf_op | source)
XLA Modules:
  0.0 94.8 jit_solution(13563701177022067175)
XLA Ops:
  0.0 3.5 %shard_map.46 = (f32[16,128,128]{2,1,0:T(8,128)S(1)}, f32[128,2048]{1,0:T(8,128)S(1)}, bf16[128,2048]{1,0:T(8,128)(2,1)S(1)}) custom-call(bf16[128,2048]{1,0:T(8,128)(2,1)} %keys_ref.1, bf16[128,2048]{1,0:T(8,128)(2,1)} %values_ref.1, bf16[128,2048]{1,0:T(8,128)(2,1)} %queries_ref.1), custom_call_target="tpu_custom_call" | custom-call | tf_op jit(solution)/shard_map/pallas_call | solution.py:226
  3.5 40.5 %all_to_all.15.parts_ref = f32[64,32,128]{2,1,0:T(8,128)S(1)} all-to-all(f32[64,32,128]{2,1,0:T(8,128)S(1)} %bitcast.4), channel_id=1, replica_groups=mesh['y2'=2,'y1'=2,'y0'=2,'x1'=2,'x0'=2,'core'=2,'z2'=2,'z1'=2,'z0'=2] {..., dimensions={0} | all-to-all | bytes 2097152 | tf_op jit(solution)/shard_map/all_to_all | solution.py:239
  44.0 0.1 shard_map.47
  44.1 13.4 %all_to_all.16.planes_ref = f32[8,32,128]{2,1,0:T(8,128)S(1)} all-to-all(f32[8,32,128]{2,1,0:T(8,128)S(1)} %shard_map.47), channel_id=1, replica_groups=mesh['y2'=2,'y1'=2,'y0'=2,'x1'=2,'x0'=2,'core'=2,'z2'=2,'z1'=2,'z0'=2] {..., dimensions={0} | all-to-all | bytes 262144 | tf_op jit(solution)/shard_map/all_to_all | solution.py:241
  57.6 0.1 shard_map.48
  57.6 0.0 copy-start
  57.7 0.0 copy-start.1
  57.7 0.0 copy-start.2
  57.7 0.0 copy-start.3
  57.7 35.7 %all_to_all.17 = f32[64,32,128]{2,1,0:T(8,128)S(1)} all-to-all(f32[64,32,128]{2,1,0:T(8,128)S(1)} %shard_map.48), channel_id=1, replica_groups=mesh['y2'=2,'y1'=2,'y0'=2,'x1'=2,'x0'=2,'core'=2,'z2'=2,'z1'=2,'z0'=2] {..., dimensions={0} | all-to-all | bytes 2097152 | tf_op jit(solution)/shard_map/all_to_all | solution.py:243
  93.4 0.0 copy-done
  93.4 0.0 copy-done.1
  93.4 0.0 copy-done.2
  93.4 0.0 copy-done.3
  93.4 1.5 %shard_map.49 = bf16[128,2048]{1,0:T(8,128)(2,1)} custom-call(bf16[128,2048]{1,0:T(8,128)(2,1)S(1)} %copy-done, bf16[128,2048]{1,0:T(8,128)(2,1)S(1)} %copy-done.1, bf16[128,2048]{1,0:T(8,128)(2,1)S(1)} %copy-done.2, f32[1,2048]{1,0:T(1,128)S(1)} %bitcast.5, f32[16,128,128]{2,1,0:T(8,128)S(1)} %bitcast.3, f32[128,2048]{1,0:T(8,128)S(1)} %get-tuple-element.9.inner_ref, ...), custom_call_target="tpu_custom_call" | custom-call | tf_op jit(solution)/shard_map/pallas_call | solution.py:244
Async XLA Ops:
  57.6 35.7 %copy-start = (bf16[128,2048]{1,0:T(8,128)(2,1)S(1)}, bf16[128,2048]{1,0:T(8,128)(2,1)}, u32[]{:S(2)}) copy-start(bf16[128,2048]{1,0:T(8,128)(2,1)} %queries_ref.1) | copy-start | bytes 1572868
  57.7 35.7 %copy-start.1 = (bf16[128,2048]{1,0:T(8,128)(2,1)S(1)}, bf16[128,2048]{1,0:T(8,128)(2,1)}, u32[]{:S(2)}) copy-start(bf16[128,2048]{1,0:T(8,128)(2,1)} %keys_ref.1) | copy-start | bytes 1572868
  57.7 35.7 %copy-start.2 = (bf16[128,2048]{1,0:T(8,128)(2,1)S(1)}, bf16[128,2048]{1,0:T(8,128)(2,1)}, u32[]{:S(2)}) copy-start(bf16[128,2048]{1,0:T(8,128)(2,1)} %values_ref.1) | copy-start | bytes 1572868
  57.7 35.7 %copy-start.3 = (f32[2048]{0:T(1024)S(1)}, f32[2048]{0:T(1024)}, u32[]{:S(2)}) copy-start(f32[2048]{0:T(1024)} %param.7) | copy-start | bytes 24580

commit v6 on v5

--- a/solution.py
+++ b/solution.py
@@ -24,7 +24,7 @@
     return index
 
 
-TOGETHER = 8
+TOGETHER = 4
 LIMIT = 16 * 2**20
 
 

time: 95.2 us -> 95.1 us (level)
  no operation moved by 1% of the time
where the time goes in v6:
time: 95.1 us; the launch traced here: 94.8 us
  blocking collectives  89.5 us (94%)
  Pallas kernels  5.27 us (6%)
    all_to_all x1, blocking collectives, local(): lax.all_to_all(state.reshape(group, piece, DK), PLANE, 0, 0, tiled=True)  40.4 us
    all_to_all x1, blocking collectives, local(): prefix = lax.all_to_all(prefix, PLANE, 0, 0, tiled=True).reshape(H, DK, DK)  35.7 us
    all_to_all x1, blocking collectives, local(): totals = lax.all_to_all(totals, ROWS, 0, 0, tiled=True)  13.4 us
    pallas_call x1, Pallas kernels, local(): pl.pallas_call(state_kernel, out_shape=[jax.ShapeDtypeStruct((H, DK, DK),...  3.67 us

profile of v6, /device:TPU:1, one launch (start us, length us, event | category | flops | bytes accessed | tf_op | source)
XLA Modules:
  0.0 94.8 jit_solution(5874463752780617270)
XLA Ops:
  0.0 3.7 %shard_map.46 = (f32[16,128,128]{2,1,0:T(8,128)S(1)}, f32[128,2048]{1,0:T(8,128)S(1)}, bf16[128,2048]{1,0:T(8,128)(2,1)S(1)}) custom-call(bf16[128,2048]{1,0:T(8,128)(2,1)} %keys_ref.1, bf16[128,2048]{1,0:T(8,128)(2,1)} %values_ref.1, bf16[128,2048]{1,0:T(8,128)(2,1)} %queries_ref.1), custom_call_target="tpu_custom_call" | custom-call | tf_op jit(solution)/shard_map/pallas_call | solution.py:226
  3.7 40.4 %all_to_all.15.parts_ref = f32[64,32,128]{2,1,0:T(8,128)S(1)} all-to-all(f32[64,32,128]{2,1,0:T(8,128)S(1)} %bitcast.4), channel_id=1, replica_groups=mesh['y2'=2,'y1'=2,'y0'=2,'x1'=2,'x0'=2,'core'=2,'z2'=2,'z1'=2,'z0'=2] {..., dimensions={0} | all-to-all | bytes 2097152 | tf_op jit(solution)/shard_map/all_to_all | solution.py:239
  44.0 0.1 shard_map.47
  44.1 13.4 %all_to_all.16.planes_ref = f32[8,32,128]{2,1,0:T(8,128)S(1)} all-to-all(f32[8,32,128]{2,1,0:T(8,128)S(1)} %shard_map.47), channel_id=1, replica_groups=mesh['y2'=2,'y1'=2,'y0'=2,'x1'=2,'x0'=2,'core'=2,'z2'=2,'z1'=2,'z0'=2] {..., dimensions={0} | all-to-all | bytes 262144 | tf_op jit(solution)/shard_map/all_to_all | solution.py:241
  57.6 0.1 shard_map.48
  57.6 0.0 copy-start
  57.7 0.0 copy-start.1
  57.7 0.0 copy-start.2
  57.7 0.0 copy-start.3
  57.7 35.7 %all_to_all.17 = f32[64,32,128]{2,1,0:T(8,128)S(1)} all-to-all(f32[64,32,128]{2,1,0:T(8,128)S(1)} %shard_map.48), channel_id=1, replica_groups=mesh['y2'=2,'y1'=2,'y0'=2,'x1'=2,'x0'=2,'core'=2,'z2'=2,'z1'=2,'z0'=2] {..., dimensions={0} | all-to-all | bytes 2097152 | tf_op jit(solution)/shard_map/all_to_all | solution.py:243
  93.4 0.0 copy-done
  93.4 0.0 copy-done.1
  93.4 0.0 copy-done.2
  93.4 0.0 copy-done.3
  93.4 1.4 %shard_map.49 = bf16[128,2048]{1,0:T(8,128)(2,1)} custom-call(bf16[128,2048]{1,0:T(8,128)(2,1)S(1)} %copy-done, bf16[128,2048]{1,0:T(8,128)(2,1)S(1)} %copy-done.1, bf16[128,2048]{1,0:T(8,128)(2,1)S(1)} %copy-done.2, f32[1,2048]{1,0:T(1,128)S(1)} %bitcast.5, f32[16,128,128]{2,1,0:T(8,128)S(1)} %bitcast.3, f32[128,2048]{1,0:T(8,128)S(1)} %get-tuple-element.9.inner_ref, ...), custom_call_target="tpu_custom_call" | custom-call | tf_op jit(solution)/shard_map/pallas_call | solution.py:244
Async XLA Ops:
  57.6 35.7 %copy-start = (bf16[128,2048]{1,0:T(8,128)(2,1)S(1)}, bf16[128,2048]{1,0:T(8,128)(2,1)}, u32[]{:S(2)}) copy-start(bf16[128,2048]{1,0:T(8,128)(2,1)} %queries_ref.1) | copy-start | bytes 1572868
  57.7 35.7 %copy-start.1 = (bf16[128,2048]{1,0:T(8,128)(2,1)S(1)}, bf16[128,2048]{1,0:T(8,128)(2,1)}, u32[]{:S(2)}) copy-start(bf16[128,2048]{1,0:T(8,128)(2,1)} %keys_ref.1) | copy-start | bytes 1572868
  57.7 35.7 %copy-start.2 = (bf16[128,2048]{1,0:T(8,128)(2,1)S(1)}, bf16[128,2048]{1,0:T(8,128)(2,1)}, u32[]{:S(2)}) copy-start(bf16[128,2048]{1,0:T(8,128)(2,1)} %values_ref.1) | copy-start | bytes 1572868
  57.7 35.7 %copy-start.3 = (f32[2048]{0:T(1024)S(1)}, f32[2048]{0:T(1024)}, u32[]{:S(2)}) copy-start(f32[2048]{0:T(1024)} %param.7) | copy-start | bytes 24580
